TPU v7x, 1024 devices: a whole 8x8x8 slice. The times are simulated.
1024 devices in a mesh: dp: 64 (over z, x), tensor: 16 (over y, core).
Axes of the slice: x: 8, y: 8, z: 8, core: 2. Of those that a mesh axis runs over, the one named last changes fastest.
Arguments:
- masters: float32 [16, 64, 38400], P('tensor', 'dp'), may hold values from -0.078125 to 0.078125
- offsets: int32 [65], replicated, may hold values from 0 to 1638400, as said below
- tokens: bfloat16 [2, 64, 64, 5120], P(None, 'dp'), may hold values from -6 to 6
- lengths: int32 [64, 64], P('dp'), may hold values from 2 to 256, as said below
- cache_keys: bfloat16 [64, 16, 16, 256, 128], P('dp', 'tensor')
- cache_values: bfloat16 [64, 16, 16, 256, 128], P('dp', 'tensor'), may hold values from -6 to 6
Outputs:
- attended: bfloat16 [2, 64, 16, 16, 1024], P(None, 'dp', 'tensor')
- new_entries: bfloat16 [2, 64, 16, 16, 256], P(None, 'dp', 'tensor')
Inputs may be any that keep to these rules, and one draw needn't show every extreme that they name: offsets[0] = 0 and offsets[64] = 1638400; every offset is a multiple of 128; offsets[p] lies within 6400 of p * 25600; in every draw some piece is exactly 38400 long. `lengths`: in every group some row has exactly 256 cached positions.
All inputs are finite; a program needn't handle non-finite values.
Results may differ from a plain program's by a relative error of at most 0.011.
Values may be sent and summed in bfloat16 or wider, within the bound.
A program may use at most 32 MiB of HBM per device.

v0:
```python
import math

import jax
import jax.numpy as jnp
from jax import lax
from jax.sharding import PartitionSpec as P

D = 5120
HD = 128
QH_DEV = 2
GQ = 8
GRAIN = 128


ROPE_BASE = 1000000.0


def swapped(value, axis, stride):
    return lax.ppermute(value, axis, [(i, i ^ 1 << stride) for i in range(lax.axis_size(axis))])


def rotate(values, positions, freq_index):
    half = values.shape[-1] // 2
    inverse = jnp.exp(freq_index.astype(jnp.float32) * (-2.0 * math.log(ROPE_BASE) / HD))
    angles = positions * inverse
    cosine = jnp.cos(angles)
    sine_part = jnp.sin(angles)
    leading = values[..., :half]
    trailing = values[..., half:]
    return jnp.concatenate(
        [leading * cosine - trailing * sine_part, trailing * cosine + leading * sine_part], axis=-1
    )


def attend(queries, keys, values, new_keys, new_values, row_lengths):
    score_scale = HD ** (-0.5)
    cache_scores = (
        jnp.einsum("sigh,ilh->sigl", queries, keys, preferred_element_type=jnp.float32)
        * score_scale
    )
    live_mask = jnp.arange(keys.shape[1], dtype=jnp.int32)[None, :] < row_lengths[:, None]
    cache_scores = jnp.where(live_mask[None, :, None, :], cache_scores, -jnp.inf)
    own_scores = (
        jnp.einsum("sigh,jih->sigj", queries, new_keys, preferred_element_type=jnp.float32)
        * score_scale
    )
    allowed = jnp.arange(2, dtype=jnp.int32)[None, :] <= jnp.arange(2, dtype=jnp.int32)[:, None]
    own_scores = jnp.where(allowed[:, None, None, :], own_scores, -jnp.inf)
    row_top = jnp.maximum(
        jnp.max(cache_scores, axis=-1, keepdims=True), jnp.max(own_scores, axis=-1, keepdims=True)
    )
    cache_exp = jnp.exp(cache_scores - row_top)
    own_exp = jnp.exp(own_scores - row_top)
    denominator = jnp.sum(cache_exp, axis=-1, keepdims=True) + jnp.sum(
        own_exp, axis=-1, keepdims=True
    )
    cache_weights = (cache_exp / denominator).astype(jnp.bfloat16)
    own_weights = (own_exp / denominator).astype(jnp.bfloat16)
    mixed = jnp.einsum("sigl,ilh->sigh", cache_weights, values, preferred_element_type=jnp.float32)
    mixed = mixed + jnp.einsum(
        "sigj,jih->sigh", own_weights, new_values, preferred_element_type=jnp.float32
    )
    return mixed.astype(jnp.bfloat16)


def split_rows(arrays, quarter, bit_number):
    row_axis = 2 - bit_number
    side_bit = quarter // (1 << bit_number) % 2
    kept = [lax.dynamic_index_in_dim(part, side_bit, row_axis, keepdims=False) for part in arrays]
    sent = [
        lax.dynamic_index_in_dim(part, 1 - side_bit, row_axis, keepdims=False) for part in arrays
    ]
    return (kept, sent, side_bit)


def join_rows(kept, received, side_bit):
    return [
        jnp.where(
            side_bit == 0,
            jnp.concatenate([own_part, theirs], axis=-1),
            jnp.concatenate([theirs, own_part], axis=-1),
        )
        for own_part, theirs in zip(kept, received)
    ]


def per_device(masters, offsets, tokens, lengths, cache_keys, cache_values):
    own_piece = masters.reshape(-1).astype(jnp.bfloat16)
    capacity = own_piece.shape[0]
    cap_rows = capacity // GRAIN
    own_rows = own_piece.reshape(cap_rows, GRAIN)
    dp_count = lax.axis_size("dp")
    query_width = QH_DEV * HD
    entry_count = D * (query_width + HD // 2)
    gathered = lax.all_gather(own_rows, "dp", axis=0, tiled=True)
    row_starts = jnp.arange(entry_count // GRAIN, dtype=jnp.int32) * GRAIN
    inner_bounds = offsets[1:dp_count]
    owner_index = jnp.sum((inner_bounds[None, :] <= row_starts[:, None]).astype(jnp.int32), axis=1)
    owner_start = jnp.take(offsets, owner_index)
    source_rows = owner_index * cap_rows + (row_starts - owner_start) // GRAIN
    flat_weights = jnp.take(gathered, source_rows, axis=0).reshape(-1)
    query_weight = flat_weights[: D * query_width].reshape(D, query_width)
    quarter_weight = flat_weights[D * query_width :].reshape(2, D, HD // 4)
    inputs = tokens[:, 0]
    group_rows = inputs.shape[1]
    row_count = cache_keys.shape[2]
    row_lengths = lengths[0]
    quarter = lax.axis_index("tensor") % 4
    positions = (row_lengths[None, :] + jnp.arange(2, dtype=jnp.int32)[:, None]).astype(jnp.float32)
    projected = jnp.einsum("srd,dc->src", inputs, query_weight, preferred_element_type=jnp.float32)
    projected = projected.reshape(2, group_rows, QH_DEV, HD)
    queries = rotate(
        projected, positions[:, :, None, None], jnp.arange(HD // 2, dtype=jnp.int32)
    ).astype(jnp.bfloat16)
    queries = queries.reshape(2, 2, 2, row_count, query_width)
    own_lengths = lax.dynamic_slice_in_dim(row_lengths, quarter * row_count, row_count)
    own_positions = lax.dynamic_slice_in_dim(positions, quarter * row_count, row_count, axis=1)
    assembled = quarter_weight[None]
    for bit_number in range(2):
        partner = swapped(assembled, "tensor", bit_number)
        side_bit = quarter // (1 << bit_number) % 2
        assembled = jnp.where(
            side_bit == 0,
            jnp.concatenate([assembled, partner], axis=0),
            jnp.concatenate([partner, assembled], axis=0),
        )
    own_inputs = lax.dynamic_slice_in_dim(inputs, quarter * row_count, row_count, axis=1)
    quarters = jnp.einsum(
        "srd,qkdc->srqkc", own_inputs, assembled, preferred_element_type=jnp.float32
    )
    freq_quarter = (
        jnp.arange(4, dtype=jnp.int32)[:, None] * (HD // 8)
        + jnp.arange(HD // 8, dtype=jnp.int32)[None, :]
    )
    rotated = rotate(quarters[:, :, :, 0, :], own_positions[:, :, None, None], freq_quarter)
    quarters = jnp.stack([rotated, quarters[:, :, :, 1, :]], axis=3).astype(jnp.bfloat16)
    arrays = [queries]
    for bit_number in range(2):
        kept, sent, side_bit = split_rows(arrays, quarter, bit_number)
        received = [swapped(sent[0], "tensor", bit_number)]
        arrays = join_rows(kept, received, side_bit)
    own_queries = arrays[0]
    fresh = (
        quarters.reshape(2, row_count, 4, 2, 2, HD // 8)
        .transpose(0, 1, 3, 4, 2, 5)
        .reshape(2, row_count, 2, HD)
    )
    own_queries = own_queries.reshape(2, row_count, GQ, HD)
    mixed = attend(
        own_queries,
        cache_keys[0, 0],
        cache_values[0, 0],
        fresh[:, :, 0, :],
        fresh[:, :, 1, :],
        own_lengths,
    )
    return (mixed.reshape(2, 1, 1, row_count, GQ * HD), fresh.reshape(2, 1, 1, row_count, 2 * HD))


def solution(mesh):
    return jax.shard_map(
        per_device,
        mesh=mesh,
        in_specs=(
            P("tensor", "dp", None),
            P(),
            P(None, "dp", None, None),
            P("dp", None),
            P("dp", "tensor", None, None, None),
            P("dp", "tensor", None, None, None),
        ),
        out_specs=(P(None, "dp", "tensor", None, None), P(None, "dp", "tensor", None, None)),
        check_vma=False,
    )
```

profile of v0, /device:TPU:1, one launch (start us, length us, event | category | flops | bytes accessed | tf_op | source)
XLA Modules:
  0.0 231.7 jit_solution(5843410432497702134)
XLA Ops:
  7.2 0.0 copy-start
  7.2 0.0 copy-start.1
  7.2 0.0 all-gather.3.cloned.1.call-start
  7.2 2.0 convert_reduce_fusion.1
  9.3 0.0 all-gather.3.cloned.1.call-update
  9.3 0.7 slice.36
  10.1 0.5 convert_reduce_fusion
  10.6 0.2 fusion.35
  10.7 0.0 copy-done.1
  10.8 0.0 copy-start.5
  10.8 71.3 %gather_fusion = s32[12800]{0:T(1024)S(1)} fusion(s32[65]{0:T(128)S(1)} %copy-done.1, s32[13312]{0:T(1024)S(1)} %pad_clamp_fusion.1), kind=kCustom, calls=%fused_computation | custom fusion | bytes 153600 | tf_op jit(solution)/shard_map/jit(_take)/gather | solution.py:99
  82.1 0.5 fusion.33
  82.7 0.0 copy-done.5
  82.7 0.1 fusion.40
  82.8 0.1 multiply_exponential_fusion
  82.9 0.1 compare_and_fusion
  83.0 34.1 %all-gather.3.cloned.1.call-done = bf16[64,300,128]{2,1,0:T(8,128)(2,1)} async-done(((bf16[1,300,128]{2,1,0:T(8,128)(2,1)}), bf16[64,300,128]{2,1,0:T(8,128)(2,1)}) %all-gather.3.cloned.1.call-update) | async-done | bytes 4915216 | tf_op jit(solution)/shard_map/all_gather | solution.py:95
  117.1 7.2 %reshape.291 = bf16[19200,128]{1,0:T(8,128)(2,1)} reshape(bf16[64,300,128]{2,1,0:T(8,128)(2,1)} %all-gather.3.cloned.1.call-done) | data formatting | bytes 9830400
  124.3 27.2 %gather_fusion.1 = bf16[12800,128]{1,0:T(8,128)(2,1)} fusion(bf16[19200,128]{1,0:T(8,128)(2,1)} %reshape.291, s32[13312]{0:T(1024)S(1)} %pad_clamp_fusion), kind=kCustom, calls=%fused_computation.1 | custom fusion | bytes 6604800 | tf_op jit(solution)/shard_map/jit(_take)/gather | solution.py:101
  151.5 8.6 %broadcast_select_fusion = bf16[12800,128]{1,0:T(8,128)(2,1)S(1)} fusion(bf16[12800,128]{1,0:T(8,128)(2,1)} %gather_fusion.1, pred[12800]{0:T(1024)(128)(4,1)S(1)} %compare_and_fusion), kind=kLoop, calls=%fused_computation.3 | loop fusion | flops 1638400 | bytes 6566400 | tf_op jit(solution)/shard_map/jit(_take)/select_n | solution.py:101
  160.1 0.0 copy-start.2
  160.1 1.7 copy-done.2
  161.8 2.2 broadcast_in_dim_reshape.3
  164.0 3.0 %copy.33 = bf16[1,2,5120,32]{2,3,1,0:T(8,128)(2,1)S(1)} copy(bf16[1,2,5120,32]{3,2,1,0:T(8,128)(2,1)} %broadcast_in_dim_reshape.3) | data formatting | bytes 1310720 | tf_op jit(solution)/shard_map/broadcast_in_dim;reshape | solution.py:118
  167.0 5.5 %collective-permute-start.2 = (bf16[1,2,5120,32]{2,3,1,0:T(8,128)(2,1)S(1)}, bf16[1,2,5120,32]{2,3,1,0:T(8,128)(2,1)}, u32[]{:S(2)}, u32[]{:S(2)}) collective-permute-start(bf16[1,2,5120,32]{2,3,1,0:T(8,128)(2,1)S(1)} %copy.33), channel_id=1, source_target_pairs={{0,1},{1,0},{2,3},{3,2},{4,5},{5,4},{6,7},{7,6},{8,9},{9,8},{10,11... | collective-permute-start | bytes 1966088 | tf_op jit(solution)/shard_map/ppermute | solution.py:19
  172.5 0.1 iota_compare_fusion
  172.6 0.3 multiply_cosine_fusion.1
  172.9 2.9 %slice.51 = bf16[10240,128]{1,0:T(8,128)(2,1)} slice(bf16[12800,128]{1,0:T(8,128)(2,1)} %copy-done.2), slice={[0:10240], [0:128]} | slice | bytes 5242880 | tf_op jit(solution)/shard_map/slice | solution.py:102
  175.8 5.0 %reshape.293 = bf16[5120,256,1]{1,0,2:T(8,128)(2,1)} reshape(bf16[10240,128]{1,0:T(8,128)(2,1)} %slice.51) | data formatting | bytes 5242880 | tf_op jit(solution)/shard_map/reshape | solution.py:102
  180.9 0.0 collective-permute-done.2
  180.9 1.6 maximum_select_fusion.1
  182.5 3.2 %collective-permute-start.3 = (bf16[2,2,5120,32]{2,3,1,0:T(8,128)(2,1)S(1)}, bf16[2,2,5120,32]{2,3,1,0:T(8,128)(2,1)}, u32[]{:S(2)}, u32[]{:S(2)}) collective-permute-start(bf16[2,2,5120,32]{2,3,1,0:T(8,128)(2,1)S(1)} %maximum_select_fusion.1), channel_id=1, source_target_pairs={{0,2},{1,3},{2,0},{3,1},{4,6},{5,7},{6,4},{7,5},{8,10},{9,11},{10,... | collective-permute-start | bytes 3932168 | tf_op jit(solution)/shard_map/ppermute | solution.py:19
  185.7 0.0 copy-done
  185.7 0.0 copy-done.3
  185.7 0.5 fusion.9
  186.2 0.1 reshape.271
  186.3 0.3 subtract_convert_fusion
  186.6 0.2 pad_maximum_fusion
  186.9 2.2 collective-permute-start
  189.1 0.1 constant_dynamic-slice_fusion
  189.2 0.8 collective-permute-done
  190.0 0.1 broadcast_select_fusion.1
  190.1 0.1 constant_dynamic-slice_fusion.1
  190.2 2.1 collective-permute-start.1
  192.4 23.2 %collective-permute-done.1 = bf16[2,16,512]{2,0,1:T(2,128)(2,1)S(1)} collective-permute-done((bf16[2,16,512]{2,0,1:T(2,128)(2,1)S(1)}, bf16[2,16,512]{2,0,1:T(2,128)(2,1)S(1)}, u32[]{:S(2)}, u32[]{:S(2)}) %collective-permute-start.1) | collective-permute-done | bytes 32800 | tf_op jit(solution)/shard_map/ppermute | solution.py:19
  215.6 1.7 fusion.44
  217.3 0.0 collective-permute-done.3
  217.4 3.6 %fusion.1 = f32[2,16,4,2,32]{4,1,3,2,0:T(8,128)S(1)} fusion(bf16[2,2,5120,32]{2,3,1,0:T(8,128)(2,1)} %collective-permute-done.3, bf16[2,2,5120,32]{2,3,1,0:T(8,128)(2,1)S(1)} %maximum_select_fusion.1, pred[]{:T(512)S(6)} %eq.14, bf16[2,1,64,5120]{3,2,1,0:T(8,128)(2,1)S(1)} %copy-done, s32[]{:T(128)S(6)} %select_n.161), kind=kOutput, calls=%fused_computation.6 | convolution fusion | flops 95682560 | bytes 2981893 | tf_op jit(solution)/shard_map/srd,qkdc->srqkc/dot_general | solution.py:128
  221.0 0.0 copy-start.4
  221.0 0.1 stack.9
  221.1 0.3 fusion.27
  221.4 0.1 pad_maximum_fusion.1
  221.5 0.1 stack.8
  221.6 0.2 maximum_bitcast_fusion
  221.8 0.1 copy.35
  221.9 0.1 copy.36
  222.0 0.1 reshape.272
  222.1 0.4 fusion.45
  222.6 0.2 fusion.19
  222.8 0.1 fusion.36
  222.9 0.2 convolution_bitcast_fusion.1
  223.1 0.3 fusion.12
  223.5 0.6 copy.37
  224.1 0.8 reshape_reshape.3
  (21 shorter events, 0.4 us)
Async XLA Ops:
  7.2 178.5 %copy-start = (bf16[2,1,64,5120]{3,2,1,0:T(8,128)(2,1)S(1)}, bf16[2,1,64,5120]{3,2,1,0:T(8,128)(2,1)}, u32[]{:S(2)}) copy-start(bf16[2,1,64,5120]{3,2,1,0:T(8,128)(2,1)} %param.8) | copy-start | bytes 3932164
  7.2 3.6 %copy-start.1 = (s32[65]{0:T(128)S(1)}, s32[65]{0:T(128)}, u32[]{:S(2)}) copy-start(s32[65]{0:T(128)} %param.7) | copy-start | bytes 784
  7.2 109.9 %all-gather.3.cloned.1.call-start = ((), (), s32[]{:S(2)}) async-start(), calls=%async_computation | async-start | bytes 5058560 | tf_op jit(solution)/shard_map/all_gather | solution.py:95
  10.8 71.9 %copy-start.5 = (s32[1,64]{1,0:T(1,128)S(1)}, s32[1,64]{1,0:T(1,128)}, u32[]{:S(2)}) copy-start(s32[1,64]{1,0:T(1,128)} %param.9) | copy-start | bytes 772
  160.1 1.7 copy-start.2
  167.0 13.9 %collective-permute-start.2 = (bf16[1,2,5120,32]{2,3,1,0:T(8,128)(2,1)S(1)}, bf16[1,2,5120,32]{2,3,1,0:T(8,128)(2,1)}, u32[]{:S(2)}, u32[]{:S(2)}) collective-permute-start(bf16[1,2,5120,32]{2,3,1,0:T(8,128)(2,1)S(1)} %copy.33), channel_id=1, source_target_pairs={{0,1},{1,0},{2,3},{3,2},{4,5},{5,4},{6,7},{7,6},{8,9},{9,8},{10,11... | collective-permute-start | bytes 1966088 | tf_op jit(solution)/shard_map/ppermute | solution.py:19
  180.9 4.8 %copy-start.3 = (bf16[5120,256,1]{1,0,2:T(8,128)(2,1)S(1)}, bf16[5120,256,1]{1,0,2:T(8,128)(2,1)}, u32[]{:S(2)}) copy-start(bf16[5120,256,1]{1,0,2:T(8,128)(2,1)} %reshape.293) | copy-start | bytes 7864324
  182.5 34.8 %collective-permute-start.3 = (bf16[2,2,5120,32]{2,3,1,0:T(8,128)(2,1)S(1)}, bf16[2,2,5120,32]{2,3,1,0:T(8,128)(2,1)}, u32[]{:S(2)}, u32[]{:S(2)}) collective-permute-start(bf16[2,2,5120,32]{2,3,1,0:T(8,128)(2,1)S(1)} %maximum_select_fusion.1), channel_id=1, source_target_pairs={{0,2},{1,3},{2,0},{3,1},{4,6},{5,7},{6,4},{7,5},{8,10},{9,11},{10,... | collective-permute-start | bytes 3932168 | tf_op jit(solution)/shard_map/ppermute | solution.py:19
  186.9 3.1 %collective-permute-start = (bf16[2,2,16,256]{3,0,2,1:T(2,128)(2,1)S(1)}, bf16[2,2,16,256]{3,0,2,1:T(2,128)(2,1)S(1)}, u32[]{:S(2)}, u32[]{:S(2)}) collective-permute-start(bf16[2,2,16,256]{3,0,2,1:T(2,128)(2,1)S(1)} %bitcast.98), channel_id=1, source_target_pairs={{0,1},{1,0},{2,3},{3,2},{4,5},{5,4},{6,7},{7,6},{8,9},{9,8},{10,11... | collective-permute-start | bytes 98312 | tf_op jit(solution)/shard_map/ppermute | solution.py:19
  190.2 25.4 %collective-permute-start.1 = (bf16[2,16,512]{2,0,1:T(2,128)(2,1)S(1)}, bf16[2,16,512]{2,0,1:T(2,128)(2,1)S(1)}, u32[]{:S(2)}, u32[]{:S(2)}) collective-permute-start(bf16[2,16,512]{2,0,1:T(2,128)(2,1)S(1)} %get-tuple-element.15), channel_id=1, source_target_pairs={{0,2},{1,3},{2,0},{3,1},{4,6},{5,7},{6,4},{7,5},{8,10},{9,11},{10,... | collective-permute-start | bytes 98312 | tf_op jit(solution)/shard_map/ppermute | solution.py:19
  221.0 2.2 copy-start.4
Sparse Core Ops, SparseCore 0:
  12.2 104.8 all-gather.2
where the time goes:
time: 233 us; the launch traced here: 232 us
  local copies, waits for them, and re-layouts  124 us (53%)
  waiting for transfers between devices  58.2 us (25%)
  other arithmetic  15.5 us (7%)
  between operations  14.5 us (6%)
  starting transfers between devices  13 us (6%)
  matrix products  6.8 us (3%)
    gather x1, local copies, waits for them, and re-layouts, per_device(): owner_start = jnp.take(offsets, owner_index)  71.3 us
    all_gather x1, waiting for transfers between devices, per_device(): gathered = lax.all_gather(own_rows, 'dp', axis=0, tiled=True)  34.1 us
    gather x1, local copies, waits for them, and re-layouts, per_device(): flat_weights = jnp.take(gathered, source_rows, axis=0).reshape(-1)  27.2 us
    ppermute x4, waiting for transfers between devices, swapped(): lax.ppermute(value, axis, [(i, i ^ 1 << stride) for i in range(lax.axis_s...  24 us
    ppermute x4, starting transfers between devices, swapped(): lax.ppermute(value, axis, [(i, i ^ 1 << stride) for i in range(lax.axis_s...  13 us
    unnamed x14, local copies, waits for them, and re-layouts  9.55 us
    select_n x2, other arithmetic, per_device(): flat_weights = jnp.take(gathered, source_rows, axis=0).reshape(-1)  9.12 us
    another operation x2, local copies, waits for them, and re-layouts, per_device(): assembled = quarter_weight[None]  5.17 us
  transfers between devices with their start and end apart: 5, of which 3 were waited for; matrix products, arithmetic and copies ran while one was open for 37% of the time, Pallas kernels for 0%

commit v1 on v0

v1 whole, which is shorter than its diff:
```python
import math

import jax
import jax.numpy as jnp
from jax import lax
from jax.experimental import pallas as pl
from jax.experimental.pallas import tpu as pltpu
from jax.sharding import PartitionSpec as P

D = 5120
HD = 128
GRAIN = 128
SIDE = 8
UNIT = 32
SLAB = 50
HALF = SLAB // 2
QUERY_UNITS = 320
KEY_UNITS = 40
ROWS = 128
FRONT = 144
ROPE_BASE = 1000000.0
MESH = pl.DeviceIdType.MESH
F32 = jnp.float32
BF16 = jnp.bfloat16
NEAR_FIRST = (1, 7, 2, 6, 3, 5, 4)


def remote(src, dst, send_sem, recv_sem, device):
    return pltpu.make_async_remote_copy(
        src_ref=src, dst_ref=dst, send_sem=send_sem, recv_sem=recv_sem, device_id=device, device_id_type=MESH
    )


def wrap(value):
    return lax.rem(value + 2 * SIDE, SIDE)


def first_unit(x):
    return 6 * x + x // 4


def either(wide, act):
    @pl.when(wide)
    def _():
        act(7)

    @pl.when(jnp.logical_not(wide))
    def _():
        act(6)


def lanes_of(shape):
    return lax.broadcasted_iota(jnp.int32, shape, len(shape) - 1)


def rows_of(shape):
    return lax.broadcasted_iota(jnp.int32, shape, len(shape) - 2)


def kernel(
    masters,
    offsets,
    tokens_in,
    lengths,
    keys_in,
    values_in,
    attended,
    new_entries,
    raw,
    staged,
    from_below,
    from_above,
    ga,
    gb,
    tokens,
    keys,
    values,
    thinned,
    position,
    tables,
    outbox,
    inbox,
    queries,
    mixed,
    load_sem,
    near_send,
    near_recv,
    light_send,
    light_recv,
    ring_send,
    ring_recv,
    swap_send,
    swap_recv,
):
    dp = lax.axis_index("dp")
    t = lax.axis_index("tensor")
    z, x = dp // SIDE, lax.rem(dp, SIDE)
    quarter = lax.rem(t, 4)
    t_base = t - quarter

    loads = [
        pltpu.make_async_copy(masters, raw.at[pl.ds(FRONT, 300)], load_sem.at[0]),
        pltpu.make_async_copy(tokens_in, tokens, load_sem.at[1]),
        pltpu.make_async_copy(keys_in, keys, load_sem.at[2]),
        pltpu.make_async_copy(values_in, values, load_sem.at[3]),
    ]
    for load in loads:
        load.start()

    barrier = pltpu.get_barrier_semaphore()
    for step in range(1, SIDE):
        pl.semaphore_signal(barrier, inc=1, device_id=(z * SIDE + wrap(x + step), t), device_id_type=MESH)
        pl.semaphore_signal(barrier, inc=1, device_id=(wrap(z + step) * SIDE + x, t), device_id_type=MESH)
    for step in range(1, 4):
        pl.semaphore_signal(barrier, inc=1, device_id=(dp, t_base + lax.rem(quarter + step, 4)), device_id_type=MESH)

    @pl.when(dp > 0)
    def _():
        pl.semaphore_signal(barrier, inc=1, device_id=(dp - 1, t), device_id_type=MESH)

    @pl.when(dp < 63)
    def _():
        pl.semaphore_signal(barrier, inc=1, device_id=(dp + 1, t), device_id_type=MESH)

    wide = lax.rem(x, 4) == 3
    count = jnp.where(wide, 7, 6)
    base = z * SLAB + first_unit(x)
    own_start = offsets[dp] // GRAIN
    own_end = offsets[dp + 1] // GRAIN
    raw[0:FRONT] = jnp.zeros((FRONT, GRAIN), F32)
    raw[FRONT + 300 : 528] = jnp.zeros((528 - FRONT - 300, GRAIN), F32)
    loads[0].wait()
    for w in range(12):
        begin = jnp.clip(FRONT + UNIT * (base - 2 + w) - own_start, 0, 494)
        for odd in range(2):
            staged[w, odd] = raw[pl.ds(begin + odd, 16, stride=2), :].astype(BF16)

    pl.semaphore_wait(barrier, 2 * (SIDE - 1) + 3 + jnp.where(dp > 0, 1, 0) + jnp.where(dp < 63, 1, 0))

    up = remote(
        staged.at[pl.ds(2 + count, 3)], from_below, near_send.at[0], near_recv.at[0], (jnp.minimum(dp + 1, 63), t)
    )
    down = remote(staged.at[pl.ds(0, 2)], from_above, near_send.at[1], near_recv.at[1], (jnp.maximum(dp - 1, 0), t))

    @pl.when(dp < 63)
    def _():
        up.start()

    @pl.when(dp > 0)
    def _():
        down.start()

    @pl.when(dp > 0)
    def _():
        up.wait_recv()

    @pl.when(dp < 63)
    def _():
        down.wait_recv()

    def settle(i):
        for odd, target in ((0, ga), (1, gb)):
            row = UNIT * (base + i) + odd + 2 * rows_of((16, GRAIN))
            entry = staged[2 + i, odd].astype(F32)
            if i < 3:
                entry = jnp.where(row < own_start, from_below[i, odd].astype(F32), entry)
            if i > 3:
                place = jnp.clip(i - count + 2, 0, 1)
                entry = jnp.where(row >= own_end, from_above[place, odd].astype(F32), entry)
            target[z, first_unit(x) + i] = entry.astype(BF16)

    for i in range(6):
        settle(i)

    @pl.when(wide)
    def _():
        settle(6)

    def piece(ref, at_z, at_x, n):
        return ref.at[at_z, pl.ds(first_unit(at_x), n)]

    def light(which, step, n, sending):
        if which == 0:
            other = wrap(x + step)
            at_x = x if sending else wrap(x - step)
            ref = piece(ga, z, at_x, n)
            device = (z * SIDE + other, t)
        else:
            at_z = z if sending else wrap(z - step)
            ref = piece(gb, at_z, x, n)
            device = (wrap(z + step) * SIDE + x, t)
        return remote(ref, ref, light_send.at[which, step], light_recv.at[which, step], device)

    def neighbour(which, way):
        move = 1 if way == 0 else -1
        return (wrap(z + move) * SIDE + x, t) if which == 0 else (z * SIDE + wrap(x + move), t)

    def spread(which, at, n):
        for way in range(2):
            ref = piece(ga, z, at, n) if which == 0 else piece(gb, at, x, n)
            remote(
                ref, ref, ring_send.at[which, way, 0, 0], ring_recv.at[which, way, 0, at // 4], neighbour(which, way)
            ).start()

    def send_own(n):
        spread(0, x, n)
        spread(1, z, n)
        for step in NEAR_FIRST:
            light(0, step, n, True).start()
            light(1, step, n, True).start()

    either(wide, send_own)

    for r in range(64):
        here = jnp.full((1, HD), lengths[0, r], jnp.int32).astype(F32)
        position[r : r + 1] = here
        position[64 + r : 65 + r] = here + 1.0
    lane = lanes_of((ROWS, HD))
    rate = -2.0 * math.log(ROPE_BASE) / HD
    angle = position[...] * jnp.exp(lax.rem(lane, 64).astype(F32) * rate)
    tables[0] = jnp.cos(angle)
    tables[1] = jnp.where(lane < 64, -1.0, 1.0) * jnp.sin(angle)
    angle = position[...] * jnp.exp((quarter * 16 + lax.rem(lane, 16)).astype(F32) * rate)
    tables[2] = jnp.cos(angle)
    tables[3] = jnp.where(lax.rem(lane, 32) < 16, -1.0, 1.0) * jnp.sin(angle)

    for step in NEAR_FIRST:
        at_x = wrap(x - step)

        def pass_a(n):
            light(0, step, n, False).wait_recv()
            spread(0, at_x, n)

        def pass_b(n):
            light(1, step, n, False).wait_recv()
            spread(1, wrap(z - step), n)

        either(lax.rem(at_x, 4) == 3, pass_a)
        either(wide, pass_b)

    loads[1].wait()

    def thin(e):
        pick = (rows_of((1024, HD)) == 8 * lanes_of((1024, HD)) + e).astype(F32).astype(BF16)
        for block in range(D // 1024):
            got = jnp.dot(tokens[:, 1024 * block : 1024 * (block + 1)], pick, preferred_element_type=F32)
            thinned[e, :, HD * block : HD * (block + 1)] = got.astype(BF16)

    def chunk(which, way, hops, part, n):
        back = hops if way == 0 else -hops
        if which == 0:
            return ga.at[wrap(z - back), pl.ds(HALF * part, HALF)]
        return gb.at[pl.ds(4 * part, 4), pl.ds(first_unit(wrap(x - back)), n)]

    def ring(which, way, hops, part, n):
        ref = chunk(which, way, hops, part, n)
        return remote(
            ref,
            ref,
            ring_send.at[which, way, hops, part],
            ring_recv.at[which, way, hops, part],
            neighbour(which, way),
        )

    def arrived(which, way, hops, part, n):
        ref = chunk(which, way, hops + 1, part, n)
        remote(
            ref, ref, ring_send.at[which, way, hops, part], ring_recv.at[which, way, hops, part], neighbour(which, way)
        ).wait_recv()

    def far_wide(way, hops):
        return lax.rem(wrap(x - (hops if way == 0 else -hops)), 4) == 3

    for hops in range(1, 4):
        for part in range(2):
            for way in range(2):
                goes_on = hops < 3 or part == way
                arrived(0, way, hops - 1, part, 0)
                if goes_on:
                    ring(0, way, hops, part, 0).start()

                def pass_column(n):
                    arrived(1, way, hops - 1, part, n)
                    if goes_on:
                        ring(1, way, hops, part, n).start()

                either(far_wide(way, hops), pass_column)
            thin(2 * (hops - 1) + part)
    thin(6)
    thin(7)
    for way in range(2):
        arrived(0, way, 3, way, 0)
        either(far_wide(way, 4), lambda n: arrived(1, way, 3, way, n))

    def tall(ref, first, units):
        flat = ref.reshape(SIDE * SLAB, 16, GRAIN)
        return flat[first : first + units].reshape(16 * units, GRAIN)

    both = jnp.concatenate([tall(ga, 0, QUERY_UNITS), tall(gb, 0, QUERY_UNITS)], axis=1)
    projected = jnp.dot(tokens[...], both, preferred_element_type=F32)
    narrow = jnp.zeros((4 * ROWS, 2 * HD), F32)
    for odd, ref in ((0, ga), (1, gb)):
        weight = jnp.concatenate(
            [tall(ref, QUERY_UNITS, KEY_UNITS), tall(ref, QUERY_UNITS + KEY_UNITS, KEY_UNITS)], axis=1
        )
        narrow += jnp.dot(thinned[4 * odd : 4 * odd + 4].reshape(4 * ROWS, D // 8), weight, preferred_element_type=F32)

    def folded(first):
        total = jnp.zeros((ROWS, HD), F32)
        for j in range(4):
            total += jnp.where(lane // 32 == j, narrow[ROWS * j : ROWS * (j + 1), first : first + HD], 0.0)
        total += pltpu.roll(total, 64, 1)
        return total + pltpu.roll(total, 32, 1)

    def placed(columns):
        other = pltpu.roll(columns, 16, 1)
        even = lax.rem(quarter, 2) == 0
        inside = lax.rem(lane, 64) // 16 == quarter
        straight = (lane < 64) == even
        return jnp.where(inside, jnp.where(straight, columns, other), 0.0)

    new_key, new_value = folded(0), folded(HD)
    new_key = new_key * tables[2] + pltpu.roll(new_key, 16, 1) * tables[3]
    tiles = []
    for head in range(2):
        part = projected[:, HD * head : HD * (head + 1)]
        tiles.append(part * tables[0] + pltpu.roll(part, 64, 1) * tables[1])
    tiles += [placed(new_key), placed(new_value)]
    for number, tile in enumerate(tiles):
        tile = tile.astype(BF16)
        for i in range(4):
            for s in range(2):
                outbox[i, number, 16 * s : 16 * s + 16] = tile[64 * s + 16 * i : 64 * s + 16 * i + 16]

    def swap(step, sending):
        target = lax.rem(quarter + step, 4)
        source = quarter if sending else lax.rem(quarter + 4 - step, 4)
        return remote(
            outbox.at[target], inbox.at[source], swap_send.at[step], swap_recv.at[step], (dp, t_base + target)
        )

    for step in range(1, 4):
        swap(step, True).start()
    inbox[quarter] = outbox[quarter]
    loads[2].wait()
    loads[3].wait()
    for step in range(1, 4):
        swap(step, False).wait_recv()

    for j in range(4):
        for head in range(2):
            for s in range(2):
                queries[pl.ds(8 * s + 2 * j + head, 16, stride=16), :] = inbox[j, head, 16 * s : 16 * s + 16].astype(F32)
    fresh = []
    for number in (2, 3):
        total = inbox[0, number].astype(F32)
        for j in range(1, 4):
            total += inbox[j, number].astype(F32)
        fresh.append(total.astype(BF16))
        for s in range(2):
            new_entries[s, :, HD * (number - 2) : HD * (number - 1)] = fresh[-1][16 * s : 16 * s + 16]
    empty = jnp.zeros((HD - 32, HD), BF16)
    fresh_keys, fresh_values = [jnp.concatenate([part, empty], axis=0) for part in fresh]
    asked = queries[...].astype(BF16)
    transposed = (((1,), (1,)), ((), ()))
    scale = HD**-0.5
    own = lax.dot_general(asked, fresh_keys, transposed, preferred_element_type=F32) * scale
    row, column = rows_of((256, HD)), lanes_of((256, HD))
    allowed = (lax.rem(column, 16) == row // 16) & (column // 16 <= lax.rem(row, 16) // 8)
    own = jnp.where(allowed, own, -1e30)
    scores = []
    for k in range(16):
        part = lax.dot_general(asked[16 * k : 16 * k + 16], keys[k], transposed, preferred_element_type=F32) * scale
        live = lanes_of((16, 256)) < lengths[0, quarter * 16 + k]
        scores.append(jnp.where(live, part, -1e30))
    scores = jnp.concatenate(scores, axis=0)
    top = jnp.maximum(jnp.max(scores, axis=1, keepdims=True), jnp.max(own, axis=1, keepdims=True))
    scores = jnp.exp(scores - top)
    own = jnp.exp(own - top)
    total = jnp.sum(scores, axis=1, keepdims=True) + jnp.sum(own, axis=1, keepdims=True)
    scores = scores.astype(BF16)
    parts = [
        jnp.dot(scores[16 * k : 16 * k + 16], values[k], preferred_element_type=F32) for k in range(16)
    ]
    result = jnp.concatenate(parts, axis=0) + jnp.dot(own.astype(BF16), fresh_values, preferred_element_type=F32)
    mixed[...] = result / total
    for s in range(2):
        for m in range(8):
            attended[s, :, HD * m : HD * (m + 1)] = mixed[pl.ds(8 * s + m, 16, stride=16), :].astype(BF16)

    @pl.when(dp < 63)
    def _():
        up.wait_send()

    @pl.when(dp > 0)
    def _():
        down.wait_send()

    def sent(n):
        for step in range(1, SIDE):
            light(0, step, n, True).wait_send()
            light(1, step, n, True).wait_send()
        for way in range(2):
            whole = ga.at[z]
            remote(whole, whole, ring_send.at[0, way, 0, 0], ring_recv.at[0, way, 0, 0], neighbour(0, way)).wait_send()
            whole = gb.at[:, pl.ds(first_unit(x), n)]
            remote(whole, whole, ring_send.at[1, way, 0, 0], ring_recv.at[1, way, 0, 0], neighbour(1, way)).wait_send()

    either(wide, sent)
    for way in range(2):
        for hops in range(1, 4):
            for part in range(2):
                if hops < 3 or part == way:
                    ring(0, way, hops, part, 0).wait_send()
                    either(far_wide(way, hops), lambda n: ring(1, way, hops, part, n).wait_send())
    for step in range(1, 4):
        swap(step, True).wait_send()


def per_device(masters, offsets, tokens, lengths, cache_keys, cache_values):
    any_space = pl.BlockSpec(memory_space=pltpu.HBM)
    scalars = pl.BlockSpec(memory_space=pltpu.SMEM)
    vector = pl.BlockSpec(memory_space=pltpu.VMEM)
    dma = pltpu.SemaphoreType.DMA
    mixed, fresh = pl.pallas_call(
        kernel,
        out_shape=(jax.ShapeDtypeStruct((2, 16, 1024), BF16), jax.ShapeDtypeStruct((2, 16, 256), BF16)),
        in_specs=[any_space, scalars, any_space, scalars, any_space, any_space],
        out_specs=(vector, vector),
        scratch_shapes=[
            pltpu.VMEM((528, GRAIN), F32),
            pltpu.VMEM((12, 2, 16, GRAIN), BF16),
            pltpu.VMEM((3, 2, 16, GRAIN), BF16),
            pltpu.VMEM((2, 2, 16, GRAIN), BF16),
            pltpu.VMEM((SIDE, SLAB, 16, GRAIN), BF16),
            pltpu.VMEM((SIDE, SLAB, 16, GRAIN), BF16),
            pltpu.VMEM((ROWS, D), BF16),
            pltpu.VMEM((16, 256, HD), BF16),
            pltpu.VMEM((16, 256, HD), BF16),
            pltpu.VMEM((8, ROWS, D // 8), BF16),
            pltpu.VMEM((ROWS, HD), F32),
            pltpu.VMEM((4, ROWS, HD), F32),
            pltpu.VMEM((4, 4, 32, HD), BF16),
            pltpu.VMEM((4, 4, 32, HD), BF16),
            pltpu.VMEM((256, HD), F32),
            pltpu.VMEM((256, HD), F32),
            dma((4,)),
            dma((2,)),
            dma((2,)),
            dma((2, SIDE)),
            dma((2, SIDE)),
            dma((2, 2, 4, 2)),
            dma((2, 2, 4, 2)),
            dma((4,)),
            dma((4,)),
        ],
        compiler_params=pltpu.CompilerParams(collective_id=0, has_side_effects=True, vmem_limit_bytes=40 * 2**20),
    )(
        masters.reshape(300, GRAIN),
        offsets,
        tokens.reshape(ROWS, D),
        lengths,
        cache_keys.reshape(16, 256, HD),
        cache_values.reshape(16, 256, HD),
    )
    return mixed.reshape(2, 1, 1, 16, 1024), fresh.reshape(2, 1, 1, 16, 256)


def solution(mesh):
    return jax.shard_map(
        per_device,
        mesh=mesh,
        in_specs=(
            P("tensor", "dp", None),
            P(),
            P(None, "dp", None, None),
            P("dp", None),
            P("dp", "tensor", None, None, None),
            P("dp", "tensor", None, None, None),
        ),
        out_specs=(P(None, "dp", "tensor", None, None), P(None, "dp", "tensor", None, None)),
        check_vma=False,
    )
```

time: 233 us -> 66.7 us (0.29)
  local copies, waits for them, and re-layouts: 124 us -> 6.31 us
  waiting for transfers between devices: 58.2 us -> 0 us
  Pallas kernels: 0 us -> 58.1 us
  other arithmetic: 15.5 us -> 1.28 us
  between operations: 14.5 us -> 0.65 us
  starting transfers between devices: 13 us -> 0 us
  matrix products: 6.8 us -> 0 us
    gather x2 -> x0, local copies, waits for them, and re-layouts: 98.5 us -> none  [the longest x1 71.3 us: per_device(): owner_start = jnp.take(offsets, owner_index)]
    pallas_call x0 -> x1, Pallas kernels: none -> 58.1 us  [per_device(): pl.pallas_call(kernel, out_shape=(jax.ShapeDtypeStruct((2, 16, 1024), BF1...]
    all_gather x1 -> x0, waiting for transfers between devices: 34.1 us -> none  [per_device(): gathered = lax.all_gather(own_rows, 'dp', axis=0, tiled=True)]
    ppermute x4 -> x0, waiting for transfers between devices: 24 us -> none  [swapped(): lax.ppermute(value, axis, [(i, i ^ 1 << stride) for i in range(lax.axis_s...]
    ppermute x4 -> x0, starting transfers between devices: 13 us -> none  [swapped(): lax.ppermute(value, axis, [(i, i ^ 1 << stride) for i in range(lax.axis_s...]
    select_n x5 -> x0, other arithmetic: 11 us -> none  [the longest x2 9.12 us: per_device(): flat_weights = jnp.take(gathered, source_rows, axis=0).reshape(-1)]
    dot_general x6 -> x0, matrix products: 6.8 us -> none  [the longest x1 3.6 us: per_device(): jnp.einsum('srd,qkdc->srqkc', own_inputs, assembled, preferred_element_ty...]
    another operation x5 -> x0, local copies, waits for them, and re-layouts: 6.11 us -> none  [the longest x2 5.17 us: per_device(): assembled = quarter_weight[None]]
  transfers between devices with their start and end apart: 5 -> 0, of which waited for: 3 -> 0; matrix products, arithmetic and copies ran while one was open for 37% -> 0% of each run, Pallas kernels for 0% -> 0%
where the time goes in v1:
time: 66.7 us; the launch traced here: 66.4 us
  Pallas kernels  58.1 us (87%)
  local copies, waits for them, and re-layouts  6.31 us (9%)
  other arithmetic  1.28 us (2%)
    pallas_call x1, Pallas kernels, per_device(): pl.pallas_call(kernel, out_shape=(jax.ShapeDtypeStruct((2, 16, 1024), BF1...  58.1 us
    unnamed x12, local copies, waits for them, and re-layouts  6.31 us

profile of v1, /device:TPU:1, one launch (start us, length us, event | category | flops | bytes accessed | tf_op | source)
XLA Modules:
  0.0 66.4 jit_solution(5594436105948397497)
XLA Ops:
  0.6 1.3 %reduce = f32[38400]{0:T(1024)S(1)} reduce(f32[1,1,38400]{2,1,0:T(1,128)} %param.6, f32[]{:T(128)} %constant.5), dimensions={0,1}, to_apply=%param.6.reduce_sub_computation | reduce | bytes 307204 | tf_op args[0]
  1.9 0.0 copy-start
  1.9 1.3 %copy-done = bf16[2,1,64,5120]{3,2,1,0:T(8,128)(2,1)S(1)} copy-done((bf16[2,1,64,5120]{3,2,1,0:T(8,128)(2,1)S(1)}, bf16[2,1,64,5120]{3,2,1,0:T(8,128)(2,1)}, u32[]{:S(2)}) %copy-start) | copy-done | bytes 1310744
  3.2 0.0 copy-start.1
  3.2 1.2 %copy-done.1 = bf16[1,1,16,256,128]{4,3,2,1,0:T(8,128)(2,1)S(1)} copy-done((bf16[1,1,16,256,128]{4,3,2,1,0:T(8,128)(2,1)S(1)}, bf16[1,1,16,256,128]{4,3,2,1,0:T(8,128)(2,1)}, u32[]{:S(2)}) %copy-start.1) | copy-done | bytes 1048600
  4.5 0.0 copy-start.2
  4.5 1.2 %copy-done.2 = bf16[1,1,16,256,128]{4,3,2,1,0:T(8,128)(2,1)S(1)} copy-done((bf16[1,1,16,256,128]{4,3,2,1,0:T(8,128)(2,1)S(1)}, bf16[1,1,16,256,128]{4,3,2,1,0:T(8,128)(2,1)}, u32[]{:S(2)}) %copy-start.2) | copy-done | bytes 1048600
  5.7 0.0 copy-start.3
  5.7 0.7 copy-done.3
  6.3 0.0 copy-start.4
  6.3 0.7 copy-done.4
  7.0 58.1 %shard_map.77 = (bf16[2,16,1024]{2,1,0:T(8,128)(2,1)S(1)}, bf16[2,16,256]{2,1,0:T(8,128)(2,1)S(1)}) custom-call(f32[300,128]{1,0:T(8,128)S(1)} %bitcast.13, s32[65]{0:T(128)S(1)} %copy-done.3, bf16[128,5120]{1,0:T(8,128)(2,1)S(1)} %bitcast.10, s32[1,64]{1,0:T(1,128)S(1)} %copy-done.4, bf16[16,256,128]{2,1,0:T(8,128)(2,1)S(1)} %bitcast.11, ...), custom_call_target="tpu_custom_call" | custom-call | tf_op jit(solution)/shard_map/pallas_call | solution.py:425
  65.1 0.6 copy.12
  65.8 0.6 copy.13
Async XLA Ops:
  1.9 1.3 %copy-start = (bf16[2,1,64,5120]{3,2,1,0:T(8,128)(2,1)S(1)}, bf16[2,1,64,5120]{3,2,1,0:T(8,128)(2,1)}, u32[]{:S(2)}) copy-start(bf16[2,1,64,5120]{3,2,1,0:T(8,128)(2,1)} %param.8) | copy-start | bytes 3932164
  3.2 1.2 %copy-start.1 = (bf16[1,1,16,256,128]{4,3,2,1,0:T(8,128)(2,1)S(1)}, bf16[1,1,16,256,128]{4,3,2,1,0:T(8,128)(2,1)}, u32[]{:S(2)}) copy-start(bf16[1,1,16,256,128]{4,3,2,1,0:T(8,128)(2,1)} %param.10) | copy-start | bytes 3145732
  4.5 1.2 %copy-start.2 = (bf16[1,1,16,256,128]{4,3,2,1,0:T(8,128)(2,1)S(1)}, bf16[1,1,16,256,128]{4,3,2,1,0:T(8,128)(2,1)}, u32[]{:S(2)}) copy-start(bf16[1,1,16,256,128]{4,3,2,1,0:T(8,128)(2,1)} %param.11) | copy-start | bytes 3145732
  5.7 0.7 copy-start.3
  6.3 0.7 copy-start.4

commit v2 on v1

--- a/solution.py
+++ b/solution.py
@@ -99,7 +99,7 @@
     t_base = t - quarter
 
     loads = [
-        pltpu.make_async_copy(masters, raw.at[pl.ds(FRONT, 300)], load_sem.at[0]),
+        pltpu.make_async_copy(masters.at[:, 0], raw.at[pl.ds(FRONT, 300)], load_sem.at[0]),
         pltpu.make_async_copy(tokens_in, tokens, load_sem.at[1]),
         pltpu.make_async_copy(keys_in, keys, load_sem.at[2]),
         pltpu.make_async_copy(values_in, values, load_sem.at[3]),
@@ -454,9 +454,9 @@
             dma((4,)),
             dma((4,)),
         ],
-        compiler_params=pltpu.CompilerParams(collective_id=0, has_side_effects=True, vmem_limit_bytes=40 * 2**20),
+        compiler_params=pltpu.CompilerParams(collective_id=0, has_side_effects=True, vmem_limit_bytes=60 * 2**20),
     )(
-        masters.reshape(300, GRAIN),
+        masters.reshape(300, 1, GRAIN),
         offsets,
         tokens.reshape(ROWS, D),
         lengths,

time: 66.7 us -> 62.1 us (0.931)
  local copies, waits for them, and re-layouts: 6.31 us -> 2.8 us
  other arithmetic: 1.28 us -> 0 us
    unnamed x12 -> x2, local copies, waits for them, and re-layouts: 6.31 us -> 2.8 us
    unnamed x1 -> x0, other arithmetic: 1.28 us -> none
where the time goes in v2:
time: 62.1 us; the launch traced here: 61.9 us
  Pallas kernels  58.5 us (94%)
  local copies, waits for them, and re-layouts  2.8 us (5%)
  between operations  0.64 us (1%)
    pallas_call x1, Pallas kernels, per_device(): pl.pallas_call(kernel, out_shape=(jax.ShapeDtypeStruct((2, 16, 1024), BF1...  58.5 us
    unnamed x2, local copies, waits for them, and re-layouts  2.8 us

profile of v2, /device:TPU:1, one launch (start us, length us, event | category | flops | bytes accessed | tf_op | source)
XLA Modules:
  0.0 61.9 jit_solution(14013392981058976133)
XLA Ops:
  0.6 58.5 %shard_map.77 = (bf16[2,16,1024]{2,1,0:T(8,128)(2,1)}, bf16[2,16,256]{2,1,0:T(8,128)(2,1)}) custom-call(f32[300,1,128]{2,1,0:T(1,128)} %bitcast.13, s32[65]{0:T(128)} %offsets.1, bf16[128,5120]{1,0:T(8,128)(2,1)} %bitcast.10, s32[1,64]{1,0:T(1,128)} %lengths.1, bf16[16,256,128]{2,1,0:T(8,128)(2,1)} %bitcast.11, bf16[16,256,128]{2,1,0:T(8,128)(2,1)} %bitcast.12), custom_call_target="tpu_custom_call" | custom-call | tf_op jit(solution)/shard_map/pallas_call | solution.py:425
  59.1 1.5 %copy.12 = bf16[2,1,1,16,1024]{4,3,2,1,0:T(8,128)(2,1)} copy(bf16[2,1,1,16,1024]{4,3,2,1,0:T(8,128)(2,1)} %bitcast.14) | data formatting | bytes 131072
  60.6 1.3 %copy.13 = bf16[2,1,1,16,256]{4,3,2,1,0:T(8,128)(2,1)} copy(bf16[2,1,1,16,256]{4,3,2,1,0:T(8,128)(2,1)} %bitcast.15) | data formatting | bytes 32768
